TPU v7x, 32 devices: a whole 2x2x4 slice. The times are simulated.
32 devices in a mesh: blk: 2 (over y), wide: 16 (over z, x, core).
Axes of the slice: x: 2, y: 2, z: 4, core: 2. Of those that a mesh axis runs over, the one named last changes fastest.
Arguments:
- series: bfloat16 [5632, 640], P(('blk', 'wide'))
- scrub_mask: int32 [640], replicated, may hold values from 0 to 1, as said below
- seed_index: int32 [256], P(('blk', 'wide')), may hold values from 0 to 5631, as said below
Outputs:
- dispersion: bfloat16 [2, 2816, 256], P(None, 'wide', 'blk')
- statistic: bfloat16 [2, 2816, 256], P(None, 'wide', 'blk')
Inputs may be any that keep to these rules, and one draw needn't show every extreme that they name: Entry i of seed_index lies among the rows (i // 8) * 176 to (i // 8 + 1) * 176 - 1, and the 8 entries of one such block are distinct. `scrub_mask`: every frame of even position is kept.
All inputs are finite; a program needn't handle non-finite values.
Results may differ from a plain program's by a relative error of at most 0.0057.
Values may be sent and summed in bfloat16 or wider, within the bound.
A program may use at most 128 MiB of HBM per device.

v0:
```python
import jax
import jax.numpy as jnp
from jax import lax
from jax.sharding import PartitionSpec as P

WIN = 60
STRIDE = 30
NWIN = 20


EPSILON = 1e-05
CLIP_LEVEL = 0.99


def shifted(block, axis, distance):
    devices = range(lax.axis_size(axis))
    route = [((i - distance) % len(devices), i) for i in devices]
    return lax.ppermute(block, axis, route)


def fisher_of(values):
    clipped = jnp.clip(values, -CLIP_LEVEL, CLIP_LEVEL)
    return 0.5 * (jnp.log(1.0 + clipped) - jnp.log(1.0 - clipped))


def prepare(raw_rows, scrub_mask):
    values = raw_rows.astype(jnp.float32)
    row_count = values.shape[0]
    weight = scrub_mask.astype(jnp.float32)
    covered = STRIDE * (NWIN + 1)
    pieces = values[:, :covered].reshape(row_count, NWIN + 1, STRIDE)
    framed = jnp.concatenate([pieces[:, :-1], pieces[:, 1:]], axis=2)
    mask_pieces = weight[:covered].reshape(NWIN + 1, STRIDE)
    mask_framed = jnp.concatenate([mask_pieces[:-1], mask_pieces[1:]], axis=1)
    valid_count = jnp.sum(mask_framed, axis=1)
    centre = jnp.sum(framed * mask_framed, axis=2) / valid_count
    centred = (framed - centre[:, :, None]) * mask_framed
    spread = jnp.sum(centred * centred, axis=2)
    windows = (centred * lax.rsqrt(spread + EPSILON)[:, :, None]).astype(jnp.bfloat16)
    total_valid = jnp.sum(weight)
    mean_all = jnp.sum(values * weight, axis=1) / total_valid
    centred_all = (values - mean_all[:, None]) * weight
    spread_all = jnp.sum(centred_all * centred_all, axis=1)
    whole_std = (centred_all * lax.rsqrt(spread_all + EPSILON)[:, None]).astype(jnp.bfloat16)
    return (windows, whole_std)


def compare(target_windows, target_whole, seed_window, seed_whole, total_valid):
    window_corr = jnp.einsum(
        "tnw,snw->nts", target_windows, seed_window, preferred_element_type=jnp.float32
    )
    fisher = fisher_of(window_corr)
    first_moment = jnp.mean(fisher, axis=0)
    second = jnp.mean(fisher * fisher, axis=0)
    dispersion = ((WIN - 3) * (second - first_moment * first_moment)).astype(jnp.bfloat16)
    static = jnp.einsum("tf,sf->ts", target_whole, seed_whole, preferred_element_type=jnp.float32)
    statistic = (jnp.sqrt(total_valid - 3.0) * fisher_of(static)).astype(jnp.bfloat16)
    return (dispersion, statistic)


def body(series, scrub_mask, seed_index):
    row_count = series.shape[0]
    local_rows = seed_index % row_count
    own_seeds = jnp.take(series, local_rows, axis=0)
    total_valid = jnp.sum(scrub_mask.astype(jnp.float32))
    target_windows, target_whole = prepare(series, scrub_mask)
    blocks = lax.axis_size("blk")
    panel_rows = lax.all_gather(own_seeds, "wide", axis=0, tiled=True)
    seed_window, seed_whole = prepare(panel_rows, scrub_mask)
    panel_size = panel_rows.shape[0]
    own_block = lax.axis_index("blk")

    def record(results, source, raw_rows):
        block_windows, block_whole = prepare(raw_rows, scrub_mask)
        dispersion, statistic = compare(
            block_windows, block_whole, seed_window, seed_whole, total_valid
        )
        return (
            lax.dynamic_update_index_in_dim(results[0], dispersion, source, 0),
            lax.dynamic_update_index_in_dim(results[1], statistic, source, 0),
        )

    empty = jnp.zeros((blocks, row_count, panel_size), jnp.bfloat16)
    own_dispersion, own_statistic = compare(
        target_windows, target_whole, seed_window, seed_whole, total_valid
    )
    results = (
        lax.dynamic_update_index_in_dim(empty, own_dispersion, own_block, 0),
        lax.dynamic_update_index_in_dim(empty, own_statistic, own_block, 0),
    )

    def advance(offset, carry):
        stored, moving = carry
        moving = shifted(moving, "blk", 1)
        stored = record(stored, (own_block - offset) % blocks, moving)
        return (stored, moving)

    results, moving = lax.fori_loop(1, blocks, advance, (results, series))
    return (results[0], results[1])


def solution(mesh):
    in_specs = (P(("blk", "wide"), None), P(), P(("blk", "wide")))
    out_specs = (P(None, "wide", "blk"), P(None, "wide", "blk"))
    return jax.shard_map(body, mesh=mesh, in_specs=in_specs, out_specs=out_specs, check_vma=False)
```

profile of v0, /device:TPU:0, one launch (start us, length us, event | category | flops | bytes accessed | tf_op | source)
XLA Modules:
  0.0 40.2 jit_solution(11988424725041002628)
XLA Ops:
  0.6 0.0 copy-start
  0.6 0.0 copy-start.3
  0.6 0.0 copy-start.4
  0.7 3.0 %collective-permute-start = (bf16[176,640]{1,0:T(8,128)(2,1)}, bf16[176,640]{1,0:T(8,128)(2,1)S(1)}, u32[]{:S(2)}, u32[]{:S(2)}) collective-permute-start(bf16[176,640]{1,0:T(8,128)(2,1)} %param.3), channel_id=1, source_target_pairs={{16,0},{0,16},{17,1},{1,17},{18,2},{2,18},{19,3},{3,19},{20,4},{4,... | collective-permute-start | bytes 675848 | tf_op jit(solution)/shard_map/while/body/eval_jaxpr/ppermute | solution.py:18
  3.7 1.0 %slice.73 = f32[176,630]{1,0:T(8,128)S(1)} slice(bf16[176,640]{1,0:T(8,128)(2,1)} %param.3), slice={[0:176], [0:630]} | slice | bytes 887040 | tf_op jit(solution)/shard_map/slice | solution.py:31
  4.7 0.0 copy-done.3
  4.7 0.1 fusion.25
  4.8 0.1 slice.62
  4.9 0.1 slice.64
  5.0 0.1 pad_maximum_fusion.3
  5.0 0.1 reduce_sum.202
  5.2 0.1 reduce_sum.203
  5.3 0.6 %convert_reduce_fusion = f32[]{:T(128)} fusion(s32[640]{0:T(1024)S(1)} %copy-done.3), kind=kLoop, calls=%fused_computation.78 | loop fusion | flops 1279 | bytes 2564 | tf_op jit(solution)/shard_map/reduce_sum | solution.py:65
  5.9 0.0 copy-done.4
  5.9 0.0 copy-done
  5.9 0.6 %gather_fusion = bf16[8,640]{1,0:T(8,128)(2,1)S(1)} fusion(bf16[176,640]{1,0:T(8,128)(2,1)S(1)} %copy-done, s32[1024]{0:T(1024)S(1)} %pad_clamp_fusion), kind=kCustom, calls=%fused_computation | custom fusion | bytes 20512 | tf_op jit(solution)/shard_map/jit(_take)/gather | solution.py:64
  6.5 0.1 broadcast_select_fusion
  6.6 22.0 %all_gather.3 = bf16[128,640]{1,0:T(8,128)(2,1)S(1)} all-gather(bf16[8,640]{1,0:T(8,128)(2,1)S(1)} %broadcast_select_fusion), channel_id=1, replica_groups=mesh['blk'=2,'wide'=16] {'wide'}, dimensions={0}, use_global_device_ids=true | all-gather | bytes 174080 | tf_op jit(solution)/shard_map/all_gather | solution.py:68
  28.7 0.1 multiply_reduce_fusion.13
  28.8 0.2 copy.12
  29.0 0.1 fusion.24
  29.1 0.2 multiply_reduce_fusion.7
  29.3 0.1 broadcast_divide_fusion.2
  29.4 0.3 multiply_reduce_fusion.6
  29.7 0.7 %broadcast_divide_fusion.5 = f32[128]{0:T(128)S(1)} fusion(f32[128]{0:T(128)S(1)} %multiply_reduce_fusion.13, f32[]{:T(128)} %convert_reduce_fusion), kind=kLoop, calls=%fused_computation.75 | loop fusion | flops 128 | bytes 1028 | tf_op jit(solution)/shard_map/div | solution.py:41
  30.4 0.2 multiply_reduce_fusion.12
  30.6 0.2 copy.11
  30.9 0.1 reshape.184
  31.6 0.0 collective-permute-done
  31.7 0.2 copy.13
  31.9 0.1 reshape.186
  32.0 0.4 fusion.22
  32.4 0.7 %multiply_reduce_fusion.3 = (f32[176,20]{0,1:T(8,128)S(1)}, f32[176,20]{0,1:T(8,128)S(1)}) fusion(f32[176,20,30]{0,2,1:T(8,128)S(1)} %get-tuple-element.47, f32[176,20,30]{0,2,1:T(8,128)S(1)} %get-tuple-element.46, f32[20,60]{1,0:T(8,128)S(1)} %pad_maximum_fusion.3, f32[176,20,30]{0,2,1:T(8,128)S(1)} %get-tuple-element.56, ...), kind=kLoop, calls=%fused_computation.10 | loop fusion | flops 1260160 | bytes 1722560 | tf_op jit(solution)/shard_map/while/body/eval_jaxpr/reduce_sum | solution.py:36
  33.1 0.1 broadcast_divide_fusion.1
  33.2 1.0 %multiply_reduce_fusion.2 = (f32[176,20]{0,1:T(8,128)S(1)}, f32[176,20]{0,1:T(8,128)S(1)}) fusion(f32[176,20,30]{0,2,1:T(8,128)S(1)} %get-tuple-element.47, f32[176,20,30]{0,2,1:T(8,128)S(1)} %get-tuple-element.46, f32[176,20]{0,1:T(8,128)S(1)} %get-tuple-element.55, f32[20,60]{1,0:T(8,128)S(1)} %pad_maximum_fusion.3, f32[176,20]{0,1:T(8,128)S(1)} %get-tuple-element.54, ...), kind=kLoop, calls=%fused_computation.8 | loop fusion | flops 2104960 | bytes 1750720 | tf_op jit(solution)/shard_map/while/body/eval_jaxpr/reduce_sum | solution.py:38
  34.2 1.6 %multiply_reduce_fusion = (f32[176,128]{1,0:T(8,128)S(1)}, f32[176,128]{1,0:T(8,128)S(1)}) fusion(f32[128,20,30]{0,2,1:T(8,128)S(1)} %get-tuple-element.51, f32[128,20,30]{0,2,1:T(8,128)S(1)} %get-tuple-element.50, f32[128,20]{0,1:T(8,128)S(1)} %add_rsqrt_fusion.2, f32[128,20]{0,1:T(8,128)S(1)} %broadcast_divide_fusion.2, ...), kind=kOutput, calls=%fused_computation.1 | convolution fusion | flops 59450624 | bytes 1692864 | tf_op jit(solution)/shard_map/while/body/eval_jaxpr/tnw,snw->nts/dot_general | solution.py:49
  35.8 1.6 %multiply_reduce_fusion.1 = (f32[176,128]{1,0:T(8,128)S(1)}, f32[176,128]{1,0:T(8,128)S(1)}) fusion(f32[128,20,30]{0,2,1:T(8,128)S(1)} %get-tuple-element.51, f32[128,20,30]{0,2,1:T(8,128)S(1)} %get-tuple-element.50, f32[128,20]{0,1:T(8,128)S(1)} %add_rsqrt_fusion.2, f32[128,20]{0,1:T(8,128)S(1)} %broadcast_divide_fusion.2, ...), kind=kOutput, calls=%fused_computation.3 | convolution fusion | flops 59450624 | bytes 1692864 | tf_op jit(solution)/shard_map/tnw,snw->nts/dot_general | solution.py:49
  37.5 0.2 multiply_reduce_fusion.9
  37.6 0.6 %broadcast_divide_fusion.3 = (f32[176]{0:T(256)S(1)}, f32[176]{0:T(256)S(1)}) fusion(f32[176]{0:T(256)S(1)} %get-tuple-element.42, f32[]{:T(128)} %convert_reduce_fusion, f32[176]{0:T(256)S(1)} %get-tuple-element.43), kind=kLoop, calls=%fused_computation.73 | loop fusion | flops 352 | bytes 2820 | tf_op jit(solution)/shard_map/while/body/eval_jaxpr/div | solution.py:41
  38.3 0.3 multiply_reduce_fusion.8
  38.8 0.0 copy-start.2
  38.8 0.4 fusion.15
  39.2 0.4 fusion.13
  39.6 0.0 copy-done.2
  39.6 0.0 copy-start.1
  39.6 0.6 %copy-done.1 = bf16[2,176,128]{2,1,0:T(8,128)(2,1)} copy-done((bf16[2,176,128]{2,1,0:T(8,128)(2,1)}, bf16[2,176,128]{2,1,0:T(8,128)(2,1)S(1)}, u32[]{:S(2)}) %copy-start.1) | copy-done | bytes 90136
  (17 shorter events, 0.3 us)
Async XLA Ops:
  0.6 5.3 %copy-start = (bf16[176,640]{1,0:T(8,128)(2,1)S(1)}, bf16[176,640]{1,0:T(8,128)(2,1)}, u32[]{:S(2)}) copy-start(bf16[176,640]{1,0:T(8,128)(2,1)} %param.3) | copy-start | bytes 675844
  0.6 4.1 %copy-start.3 = (s32[640]{0:T(1024)S(1)}, s32[640]{0:T(1024)}, u32[]{:S(2)}) copy-start(s32[640]{0:T(1024)} %param.4) | copy-start | bytes 7684
  0.6 5.2 %copy-start.4 = (s32[8]{0:T(128)S(1)}, s32[8]{0:T(128)}, u32[]{:S(2)}) copy-start(s32[8]{0:T(128)} %param.5) | copy-start | bytes 100
  0.7 31.0 %collective-permute-start = (bf16[176,640]{1,0:T(8,128)(2,1)}, bf16[176,640]{1,0:T(8,128)(2,1)S(1)}, u32[]{:S(2)}, u32[]{:S(2)}) collective-permute-start(bf16[176,640]{1,0:T(8,128)(2,1)} %param.3), channel_id=1, source_target_pairs={{16,0},{0,16},{17,1},{1,17},{18,2},{2,18},{19,3},{3,19},{20,4},{4,... | collective-permute-start | bytes 675848 | tf_op jit(solution)/shard_map/while/body/eval_jaxpr/ppermute | solution.py:18
  38.8 0.8 %copy-start.2 = (bf16[2,176,128]{2,1,0:T(8,128)(2,1)}, bf16[2,176,128]{2,1,0:T(8,128)(2,1)S(1)}, u32[]{:S(2)}) copy-start(bf16[2,176,128]{2,1,0:T(8,128)(2,1)S(1)} %fusion.19) | copy-start | bytes 270340
  39.6 0.6 %copy-start.1 = (bf16[2,176,128]{2,1,0:T(8,128)(2,1)}, bf16[2,176,128]{2,1,0:T(8,128)(2,1)S(1)}, u32[]{:S(2)}) copy-start(bf16[2,176,128]{2,1,0:T(8,128)(2,1)S(1)} %fusion.13) | copy-start | bytes 270340
where the time goes:
time: 40.4 us; the launch traced here: 40.2 us
  blocking collectives  22 us (54%)
  other arithmetic  5.68 us (14%)
  matrix products  3.99 us (10%)
  local copies, waits for them, and re-layouts  3.81 us (9%)
  starting transfers between devices  3.03 us (8%)
  between operations  1.67 us (4%)
    all_gather x1, blocking collectives, body(): panel_rows = lax.all_gather(own_seeds, 'wide', axis=0, tiled=True)  22 us
    dot_general x2, matrix products, compare(): jnp.einsum('tnw,snw->nts', target_windows, seed_window, preferred_element...  3.23 us
    ppermute x1, starting transfers between devices, shifted(): return lax.ppermute(block, axis, route)  3.03 us
    slice x6, local copies, waits for them, and re-layouts, prepare(): pieces = values[:, :covered].reshape(row_count, NWIN + 1, STRIDE)  1.68 us
    reduce_sum x2, other arithmetic, prepare(): spread = jnp.sum(centred * centred, axis=2)  1.32 us
    div x2, other arithmetic, prepare(): mean_all = jnp.sum(values * weight, axis=1) / total_valid  1.3 us
    reduce_sum x2, other arithmetic, prepare(): centre = jnp.sum(framed * mask_framed, axis=2) / valid_count  0.95 us
  transfers between devices with their start and end apart: 1, of which 0 were waited for; matrix products, arithmetic and copies ran while one was open for 13% of the time, Pallas kernels for 0%

commit v1 on v0

v1 whole, which is shorter than its diff:
```python
import functools

import jax
import jax.numpy as jnp
from jax import lax
from jax.experimental import pallas as pl
from jax.experimental.pallas import tpu as pltpu
from jax.sharding import PartitionSpec as P

WIN = 60
STRIDE = 30
NWIN = 20
EPSILON = 1e-05
CLIP_LEVEL = 0.99
LANES = 128
HALF = 64
MESH = pl.DeviceIdType.MESH
NT = (((1,), (1,)), ((), ()))


def iota(shape, dim):
    return lax.broadcasted_iota(jnp.int32, shape, dim)


def piece_of(frame):
    return (frame * 2185) >> 16


def mm(a, b):
    return jnp.dot(a, b, preferred_element_type=jnp.float32)


def log_ratio(values):
    clipped = jnp.clip(values, -CLIP_LEVEL, CLIP_LEVEL)
    return jnp.log(1.0 + clipped) - jnp.log(1.0 - clipped)


def kernel(
    n_blk, n_wide, series, mask, seed_index, dispersion, statistic,
    seed_block, panel, others, pairs, spans, seeds, seed_shift, rhs, lhs, acc1, acc2,
    seed_send, seed_recv, row_send, row_recv,
):
    rows, frames = series.shape
    own = seed_index.shape[0]
    size = n_wide * own
    low = panel.shape[2]
    high = frames - low
    me_b = lax.axis_index("blk")
    me_w = lax.axis_index("wide")

    barrier = pltpu.get_barrier_semaphore()
    for d in range(1, n_wide):
        pl.semaphore_signal(
            barrier, inc=1, device_id=(me_b, lax.rem(me_w + d, n_wide)), device_id_type=MESH
        )
    for d in range(1, n_blk):
        pl.semaphore_signal(
            barrier, inc=1, device_id=(lax.rem(me_b + d, n_blk), me_w), device_id_type=MESH
        )

    base = (me_b * n_wide + me_w) * rows
    row = iota((2 * own, rows), 0) & (own - 1)
    wanted = jnp.zeros((2 * own, rows), jnp.int32)
    for i in range(own):
        wanted = jnp.where(row == i, seed_index[i] - base, wanted)
    pick = jnp.where(iota((2 * own, rows), 1) == wanted, 1.0, 0.0).astype(jnp.bfloat16)
    picked = mm(pick, series[...])
    tail = jnp.concatenate([picked[:, low:], picked[:, : low - high]], axis=1)
    block = jnp.where(iota((2 * own, low), 0) < own, picked[:, :low], tail)
    seed_block[...] = block.astype(jnp.bfloat16)

    pl.semaphore_wait(barrier, n_wide + n_blk - 2)
    seed_copies = []
    for d in range(1, n_wide):
        copy = pltpu.make_async_remote_copy(
            src_ref=seed_block, dst_ref=panel.at[d - 1],
            send_sem=seed_send.at[d - 1], recv_sem=seed_recv.at[d - 1],
            device_id=(me_b, lax.rem(me_w + d, n_wide)), device_id_type=MESH,
        )
        copy.start()
        seed_copies.append(copy)
    row_copies = []
    for d in range(1, n_blk):
        copy = pltpu.make_async_remote_copy(
            src_ref=series, dst_ref=others.at[d - 1],
            send_sem=row_send.at[d - 1], recv_sem=row_recv.at[d - 1],
            device_id=(lax.rem(me_b + d, n_blk), me_w), device_id_type=MESH,
        )
        copy.start()
        row_copies.append(copy)

    weight = mask[...].reshape(1, frames).astype(jnp.float32)
    frame_piece = piece_of(iota((frames, 2 * LANES), 0))
    lane = iota((frames, 2 * LANES), 1)
    wanted_piece = (lane & 31) + (lane >> 7)
    pairs[...] = jnp.where(frame_piece == wanted_piece, 1.0, 0.0).astype(jnp.bfloat16)
    row_piece = piece_of(iota((frames, frames), 0))
    column_piece = piece_of(iota((frames, frames), 1))
    spans[...] = jnp.where(row_piece == column_piece, 1.0, 0.0).astype(jnp.bfloat16)
    weight_rows = jnp.broadcast_to(weight, (16, frames)).astype(jnp.bfloat16)
    counts = mm(weight_rows, pairs[...])
    count1, count2 = counts[:1, :LANES], counts[:1, LANES:]
    count = jnp.maximum(count1 + count2, 1.0)
    between = count1 * count2 / count
    count1, count2 = jnp.maximum(count1, 1.0), jnp.maximum(count2, 1.0)
    inverse_count = 1.0 / jnp.maximum(mm(weight_rows, spans[...])[:1], 1.0)
    total_valid = jnp.sum(weight, axis=1, keepdims=True)

    def stats(values):
        kept = values * weight
        kept16 = kept.astype(jnp.bfloat16)
        sums = mm(kept16, pairs[...])
        sum1, sum2 = sums[:, :LANES], sums[:, LANES:]
        inner = (values - mm(kept16, spans[...]) * inverse_count) * weight
        inner = (inner * inner).astype(jnp.bfloat16)
        inner = mm(inner, pairs[:, :LANES] + pairs[:, LANES:])
        step = sum1 / count1 - sum2 / count2
        spread = inner + between * step * step
        mean = (sum1 + sum2) / count
        mean_all = jnp.sum(kept, axis=1, keepdims=True) / total_valid
        centred = (values - mean_all) * weight
        spread_all = jnp.sum(centred * centred, axis=1, keepdims=True)
        whole = (centred * lax.rsqrt(spread_all + EPSILON)).astype(jnp.bfloat16)
        return mean, lax.rsqrt(spread + EPSILON), whole

    stat_lane = iota((rows, LANES), 1)

    def load_target(block16):
        values = block16.astype(jnp.float32)
        mean, inverse, whole = stats(values)
        inverse_high = inverse.astype(jnp.bfloat16).astype(jnp.float32)
        stat = jnp.where(
            stat_lane < 32, mean, jnp.where(stat_lane < 64, inverse_high, inverse - inverse_high)
        )
        lhs[0, :, :frames] = block16
        shift = pltpu.roll(values, frames - HALF, 1)
        lhs[1, :, :frames] = shift.astype(jnp.bfloat16)
        lhs[0, :, frames:] = stat.astype(jnp.bfloat16)
        return whole

    select_lane = iota((size, LANES), 1)
    for n in range(NWIN):
        rhs[n, size:, :LANES] = jnp.zeros((size, LANES), jnp.bfloat16)
        chosen = (select_lane == 32 + n) | (select_lane == 64 + n)
        rhs[n, size:, LANES:] = jnp.where(chosen, 1.0, 0.0).astype(jnp.bfloat16)

    own_whole = load_target(series[...])

    def unpack(block16, source):
        values = block16.astype(jnp.float32)
        at = pl.ds(pl.multiple_of(source * own, own), own)
        seeds[at, :low] = values[:own]
        seeds[at, low:] = values[own:, :high]

    unpack(seed_block[...], me_w)
    for d in range(1, n_wide):
        seed_copies[d - 1].wait_recv()
        unpack(panel[d - 1], lax.rem(me_w + n_wide - d, n_wide))

    seed_values = seeds[...]
    seed_mean, seed_inverse, seed_whole = stats(seed_values)
    seed_shift[...] = pltpu.roll(seed_values, frames - HALF, 1)
    weight_shift = pltpu.roll(jnp.broadcast_to(weight, (8, frames)), frames - HALF, 1)[:1]
    tile_lane = iota((1, LANES), 1)
    for n in range(NWIN):
        k = n * STRIDE // HALF
        at = slice(k // 2 * LANES, k // 2 * LANES + LANES)
        first = n * STRIDE - k * HALF
        inside = (tile_lane >= first) & (tile_lane < first + WIN)
        kept = jnp.where(inside, (weight_shift if k % 2 else weight)[:, at], 0.0)
        tile = (seed_shift if k % 2 else seeds)[:, at]
        window = (tile - seed_mean[:, n : n + 1]) * kept * seed_inverse[:, n : n + 1]
        window = window.astype(jnp.bfloat16)
        left = jnp.sum(window.astype(jnp.float32), axis=1, keepdims=True)
        rhs[n, :size, :LANES] = window
        rhs[n, :size, LANES:] = jnp.where(select_lane == n, -left, 0.0).astype(jnp.bfloat16)

    scale = jnp.sqrt(total_valid - 3.0) * 0.5

    def compare(whole, slot):
        static = lax.dot_general(whole, seed_whole, NT, preferred_element_type=jnp.float32)
        statistic[slot] = (scale * log_ratio(static)).astype(jnp.bfloat16)
        acc1[...] = jnp.zeros_like(acc1)
        acc2[...] = jnp.zeros_like(acc2)
        group = 4

        def step(i, carry):
            first = second = None
            for g in range(group):
                n = i * group + g
                k = n * STRIDE // HALF
                at = pl.ds(pl.multiple_of(k // 2 * LANES, LANES), LANES)
                left = jnp.concatenate([lhs[k % 2, :, at], lhs[0, :, frames:]], axis=1)
                both = lax.dot_general(left, rhs[n], NT, preferred_element_type=jnp.float32)
                z = log_ratio(both[:, :size] * both[:, size:])
                first = z if g == 0 else first + z
                second = z * z if g == 0 else second + z * z
            acc1[...] += first
            acc2[...] += second
            return carry

        lax.fori_loop(0, NWIN // group, step, 0)
        moment = acc1[...] * (0.5 / NWIN)
        spread = acc2[...] * (0.25 / NWIN) - moment * moment
        dispersion[slot] = ((WIN - 3) * spread).astype(jnp.bfloat16)

    compare(own_whole, me_b)
    for d in range(1, n_blk):
        row_copies[d - 1].wait_recv()
        whole = load_target(others[d - 1])
        compare(whole, lax.rem(me_b + n_blk - d, n_blk))

    for copy in seed_copies + row_copies:
        copy.wait_send()


def solution(mesh):
    n_blk, n_wide = mesh.shape["blk"], mesh.shape["wide"]

    def body(series, scrub_mask, seed_index):
        rows, frames = series.shape
        own = seed_index.shape[0]
        size = n_wide * own
        low = (frames // LANES + 1) // 2 * LANES
        out = jax.ShapeDtypeStruct((n_blk, rows, size), jnp.bfloat16)
        vmem = pl.BlockSpec(memory_space=pltpu.VMEM)
        return pl.pallas_call(
            functools.partial(kernel, n_blk, n_wide),
            out_shape=(out, out),
            in_specs=[vmem, vmem, pl.BlockSpec(memory_space=pltpu.SMEM)],
            out_specs=(vmem, vmem),
            scratch_shapes=[
                pltpu.VMEM((2 * own, low), jnp.bfloat16),
                pltpu.VMEM((n_wide - 1, 2 * own, low), jnp.bfloat16),
                pltpu.VMEM((n_blk - 1, rows, frames), jnp.bfloat16),
                pltpu.VMEM((frames, 2 * LANES), jnp.bfloat16),
                pltpu.VMEM((frames, frames), jnp.bfloat16),
                pltpu.VMEM((size, frames), jnp.float32),
                pltpu.VMEM((size, frames), jnp.float32),
                pltpu.VMEM((NWIN, 2 * size, 2 * LANES), jnp.bfloat16),
                pltpu.VMEM((2, rows, frames + LANES), jnp.bfloat16),
                pltpu.VMEM((rows, size), jnp.float32),
                pltpu.VMEM((rows, size), jnp.float32),
                pltpu.SemaphoreType.DMA((n_wide - 1,)),
                pltpu.SemaphoreType.DMA((n_wide - 1,)),
                pltpu.SemaphoreType.DMA((n_blk - 1,)),
                pltpu.SemaphoreType.DMA((n_blk - 1,)),
            ],
            compiler_params=pltpu.CompilerParams(
                collective_id=0, has_side_effects=True, vmem_limit_bytes=48 * 2**20
            ),
            cost_estimate=pl.CostEstimate(
                flops=n_blk * rows * size * 2 * 1800, bytes_accessed=2**20, transcendentals=0
            ),
        )(series, scrub_mask, seed_index)

    in_specs = (P(("blk", "wide"), None), P(), P(("blk", "wide")))
    out_specs = (P(None, "wide", "blk"), P(None, "wide", "blk"))
    return jax.shard_map(body, mesh=mesh, in_specs=in_specs, out_specs=out_specs, check_vma=False)
```

time: 40.4 us -> 22.5 us (0.56)
  blocking collectives: 22 us -> 0 us
  Pallas kernels: 0 us -> 17.9 us
  other arithmetic: 5.68 us -> 0 us
  matrix products: 3.99 us -> 0 us
  starting transfers between devices: 3.03 us -> 0 us
  between operations: 1.67 us -> 0.65 us
    all_gather x1 -> x0, blocking collectives: 22 us -> none  [body(): panel_rows = lax.all_gather(own_seeds, 'wide', axis=0, tiled=True)]
    pallas_call x0 -> x1, Pallas kernels: none -> 17.9 us  [body(): pl.pallas_call(functools.partial(kernel, n_blk, n_wide), out_shape=(out,...]
    dot_general x4 -> x0, matrix products: 3.99 us -> none  [the longest x2 3.23 us: compare(): jnp.einsum('tnw,snw->nts', target_windows, seed_window, preferred_element...]
    reduce_sum x12 -> x0, other arithmetic: 3.91 us -> none  [the longest x2 1.32 us: prepare(): spread = jnp.sum(centred * centred, axis=2)]
    ppermute x1 -> x0, starting transfers between devices: 3.03 us -> none  [shifted(): return lax.ppermute(block, axis, route)]
    unnamed x10 -> x8, local copies, waits for them, and re-layouts: 0.65 us -> 3.55 us
    slice x11 -> x0, local copies, waits for them, and re-layouts: 2.37 us -> none  [the longest x6 1.68 us: prepare(): pieces = values[:, :covered].reshape(row_count, NWIN + 1, STRIDE)]
    div x4 -> x0, other arithmetic: 1.45 us -> none  [the longest x2 1.3 us: prepare(): mean_all = jnp.sum(values * weight, axis=1) / total_valid]
  transfers between devices with their start and end apart: 1 -> 0, of which waited for: 0 -> 0; matrix products, arithmetic and copies ran while one was open for 13% -> 0% of each run, Pallas kernels for 0% -> 0%
where the time goes in v1:
time: 22.5 us; the launch traced here: 22.1 us
  Pallas kernels  17.9 us (80%)
  local copies, waits for them, and re-layouts  3.55 us (16%)
  between operations  0.65 us (3%)
    pallas_call x1, Pallas kernels, body(): pl.pallas_call(functools.partial(kernel, n_blk, n_wide), out_shape=(out,...  17.9 us
    unnamed x8, local copies, waits for them, and re-layouts  3.55 us

profile of v1, /device:TPU:0, one launch (start us, length us, event | category | flops | bytes accessed | tf_op | source)
XLA Modules:
  0.0 22.1 jit_solution(8972506439181552234)
XLA Ops:
  0.6 0.0 copy-start
  0.6 0.9 %copy-done = bf16[176,640]{1,0:T(8,128)(2,1)S(1)} copy-done((bf16[176,640]{1,0:T(8,128)(2,1)S(1)}, bf16[176,640]{1,0:T(8,128)(2,1)}, u32[]{:S(2)}) %copy-start) | copy-done | bytes 225304
  1.6 0.0 copy-start.1
  1.6 0.7 %copy-done.1 = s32[640]{0:T(1024)S(1)} copy-done((s32[640]{0:T(1024)S(1)}, s32[640]{0:T(1024)}, u32[]{:S(2)}) %copy-start.1) | copy-done | bytes 2584
  2.3 0.0 copy-start.2
  2.3 0.7 %copy-done.2 = s32[8]{0:T(128)S(1)} copy-done((s32[8]{0:T(128)S(1)}, s32[8]{0:T(128)}, u32[]{:S(2)}) %copy-start.2) | copy-done | bytes 56
  2.9 17.9 %shard_map.50 = (bf16[2,176,128]{2,1,0:T(8,128)(2,1)S(1)}, bf16[2,176,128]{2,1,0:T(8,128)(2,1)S(1)}) custom-call(bf16[176,640]{1,0:T(8,128)(2,1)S(1)} %copy-done, s32[640]{0:T(1024)S(1)} %copy-done.1, s32[8]{0:T(128)S(1)} %copy-done.2), custom_call_target="tpu_custom_call" | custom-call | flops 162201600 | bytes 1048576 | tf_op jit(solution)/shard_map/pallas_call | solution.py:227
  20.8 0.6 %copy.7 = bf16[2,176,128]{2,1,0:T(8,128)(2,1)} copy(bf16[2,176,128]{2,1,0:T(8,128)(2,1)S(1)} %get-tuple-element.4) | data formatting | bytes 180224
  21.4 0.6 %copy.8 = bf16[2,176,128]{2,1,0:T(8,128)(2,1)} copy(bf16[2,176,128]{2,1,0:T(8,128)(2,1)S(1)} %get-tuple-element.5) | data formatting | bytes 180224
Async XLA Ops:
  0.6 0.9 %copy-start = (bf16[176,640]{1,0:T(8,128)(2,1)S(1)}, bf16[176,640]{1,0:T(8,128)(2,1)}, u32[]{:S(2)}) copy-start(bf16[176,640]{1,0:T(8,128)(2,1)} %series.1) | copy-start | bytes 675844
  1.6 0.7 %copy-start.1 = (s32[640]{0:T(1024)S(1)}, s32[640]{0:T(1024)}, u32[]{:S(2)}) copy-start(s32[640]{0:T(1024)} %mask.1) | copy-start | bytes 7684
  2.3 0.7 %copy-start.2 = (s32[8]{0:T(128)S(1)}, s32[8]{0:T(128)}, u32[]{:S(2)}) copy-start(s32[8]{0:T(128)} %seed_index.1) | copy-start | bytes 100

commit v2 on v1

v2 whole, which is shorter than its diff:
```python
import functools

import jax
import jax.numpy as jnp
from jax import lax
from jax.experimental import pallas as pl
from jax.experimental.pallas import tpu as pltpu
from jax.sharding import PartitionSpec as P

WIN = 60
STRIDE = 30
NWIN = 20
SPAN = 21
EPSILON = 1e-05
CLIP_LEVEL = 0.99
LANES = 128
HALF = 64
MESH = pl.DeviceIdType.MESH
NT = (((1,), (1,)), ((), ()))


def iota(shape, dim):
    return lax.broadcasted_iota(jnp.int32, shape, dim)


def piece_of(frame):
    return (frame * 2185) >> 16


def mm(a, b):
    return jnp.dot(a, b, preferred_element_type=jnp.float32)


def log_ratio(values):
    clipped = jnp.clip(values, -CLIP_LEVEL, CLIP_LEVEL)
    return jnp.log(1.0 + clipped) - jnp.log(1.0 - clipped)


def split(values):
    high = values.astype(jnp.bfloat16).astype(jnp.float32)
    return high, values - high


def kernel(
    n_blk, n_wide, series_hbm, mask_hbm, seed_hbm, out,
    series, mask, seed_index, seed_block, panel, others, own_stat, other_stats, pairs, spans, seeds,
    seed_stats, across, mask_across, rhs, whole_rhs, lhs, acc1, acc2,
    load_sem, seed_send, seed_recv, row_send, row_recv, stat_send, stat_recv,
):
    rows, frames = series.shape
    own = seed_index.shape[0]
    size = n_wide * own
    low = panel.shape[2]
    high = frames - low
    me_b = lax.axis_index("blk")
    me_w = lax.axis_index("wide")

    loads = [
        pltpu.make_async_copy(seed_hbm, seed_index, load_sem.at[0]),
        pltpu.make_async_copy(mask_hbm, mask, load_sem.at[1]),
        pltpu.make_async_copy(series_hbm, series, load_sem.at[2]),
    ]
    for copy in loads:
        copy.start()
    barrier = pltpu.get_barrier_semaphore()
    for d in range(1, n_wide):
        pl.semaphore_signal(
            barrier, inc=1, device_id=(me_b, lax.rem(me_w + d, n_wide)), device_id_type=MESH
        )
    for d in range(1, n_blk):
        pl.semaphore_signal(
            barrier, inc=1, device_id=(lax.rem(me_b + d, n_blk), me_w), device_id_type=MESH
        )

    frame_piece = piece_of(iota((frames, 2 * LANES), 0))
    lane = iota((frames, 2 * LANES), 1)
    wanted_piece = (lane & 31) + (lane >> 7)
    pairs[...] = jnp.where(frame_piece == wanted_piece, 1.0, 0.0).astype(jnp.bfloat16)
    row_piece = piece_of(iota((frames, frames), 0))
    column_piece = piece_of(iota((frames, frames), 1))
    spans[...] = jnp.where(row_piece == column_piece, 1.0, 0.0).astype(jnp.bfloat16)
    for copy in loads:
        copy.wait()
    weight = mask[...].reshape(1, frames).astype(jnp.float32)
    weight_rows = jnp.broadcast_to(weight, (16, frames)).astype(jnp.bfloat16)
    counts = mm(weight_rows, pairs[...])
    count1, count2 = counts[:1, :LANES], counts[:1, LANES:]
    count = jnp.maximum(count1 + count2, 1.0)
    between = count1 * count2 / count
    count1, count2 = jnp.maximum(count1, 1.0), jnp.maximum(count2, 1.0)
    inverse_count = 1.0 / jnp.maximum(mm(weight_rows, spans[...])[:1], 1.0)
    total_valid = jnp.sum(weight, axis=1, keepdims=True)

    def stats(values):
        kept = values * weight
        kept16 = kept.astype(jnp.bfloat16)
        sums = mm(kept16, pairs[...])
        sum1, sum2 = sums[:, :LANES], sums[:, LANES:]
        inner = (values - mm(kept16, spans[...]) * inverse_count) * weight
        inner = (inner * inner).astype(jnp.bfloat16)
        inner = mm(inner, pairs[:, :LANES] + pairs[:, LANES:])
        step = sum1 / count1 - sum2 / count2
        spread = inner + between * step * step
        mean = (sum1 + sum2) / count
        mean_all = jnp.sum(kept, axis=1, keepdims=True) / total_valid
        centred = (values - mean_all) * weight
        spread_all = jnp.sum(centred * centred, axis=1, keepdims=True)
        at = iota(mean.shape, 1)
        whole = (at & 31) == SPAN
        mean_high, mean_low = split(jnp.where(whole, mean_all, mean))
        inverse = lax.rsqrt(jnp.where(whole, spread_all, spread) + EPSILON)
        inverse_high, inverse_low = split(inverse)
        means = jnp.where(at < 32, mean_high, mean_low)
        return jnp.where(at < 64, means, jnp.where(at < 96, inverse_high, inverse_low))

    base = (me_b * n_wide + me_w) * rows
    row = iota((2 * own, rows), 0) & (own - 1)
    wanted = jnp.zeros((2 * own, rows), jnp.int32)
    for i in range(own):
        wanted = jnp.where(row == i, seed_index[i] - base, wanted)
    pick = jnp.where(iota((2 * own, rows), 1) == wanted, 1.0, 0.0).astype(jnp.bfloat16)
    picked = mm(pick, series[...])
    tail = jnp.concatenate([picked[:, low:], stats(picked)], axis=1)
    block = jnp.where(iota((2 * own, low), 0) < own, picked[:, :low], tail)
    seed_block[...] = block.astype(jnp.bfloat16)

    pl.semaphore_wait(barrier, n_wide + n_blk - 2)
    seed_copies = []
    for d in range(1, n_wide):
        copy = pltpu.make_async_remote_copy(
            src_ref=seed_block, dst_ref=panel.at[d - 1],
            send_sem=seed_send.at[d - 1], recv_sem=seed_recv.at[d - 1],
            device_id=(me_b, lax.rem(me_w + d, n_wide)), device_id_type=MESH,
        )
        copy.start()
        seed_copies.append(copy)

    def to_group(source, buffer, send, recv):
        copies = []
        for d in range(1, n_blk):
            copy = pltpu.make_async_remote_copy(
                src_ref=source, dst_ref=buffer.at[d - 1],
                send_sem=send.at[d - 1], recv_sem=recv.at[d - 1],
                device_id=(lax.rem(me_b + d, n_blk), me_w), device_id_type=MESH,
            )
            copy.start()
            copies.append(copy)
        return copies

    row_copies = to_group(series, others, row_send, row_recv)

    def load_target(block16, stat):
        lhs[0, :, :frames] = block16
        shift = pltpu.roll(block16.astype(jnp.float32), frames - HALF, 1)
        lhs[1, :, :frames] = shift.astype(jnp.bfloat16)
        lhs[0, :, frames:] = stat

    own_stat[...] = stats(series[...].astype(jnp.float32)).astype(jnp.bfloat16)
    stat_copies = to_group(own_stat, other_stats, stat_send, stat_recv)
    load_target(series[...], own_stat[...])

    select = iota((LANES, size), 0)

    def choose(n):
        return jnp.where((select == 64 + n) | (select == 96 + n), 1.0, 0.0).astype(jnp.bfloat16)

    zeros = jnp.zeros((LANES, size), jnp.bfloat16)
    for n in range(NWIN):
        rhs[n, :LANES, :size] = zeros
        rhs[n, :LANES, size:] = zeros
        rhs[n, LANES:, :size] = zeros
        rhs[n, LANES:, size:] = choose(n)
    whole_rhs[:frames, size:] = jnp.zeros((frames, size), jnp.bfloat16)
    whole_rhs[frames:, size:] = choose(SPAN)
    mask_across[...] = jnp.broadcast_to(weight, (LANES, frames)).T

    def unpack(block16, source):
        values = block16.astype(jnp.float32)
        at = pl.ds(pl.multiple_of(source * own, own), own)
        seeds[at, :low] = values[:own]
        seeds[at, low:] = values[own:, :high]
        seed_stats[at, :] = values[own:, high:]

    unpack(seed_block[...], me_w)
    for d in range(1, n_wide):
        seed_copies[d - 1].wait_recv()
        unpack(panel[d - 1], lax.rem(me_w + n_wide - d, n_wide))

    across[...] = seeds[...].T
    stat_across = seed_stats[...].T
    mean_across = stat_across[:32] + stat_across[32:64]
    inverse_across = stat_across[64:96] + stat_across[96:]

    def wide_mask(a, b):
        return jnp.concatenate([mask_across[a:b, :]] * (size // LANES), axis=1)

    for n in range(NWIN):
        first = n * STRIDE
        k = first // HALF * HALF
        a, b = first // 16 * 16, -(-(first + WIN) // 16) * 16
        frame = iota((b - a, size), 0) + a
        kept = jnp.where((frame >= first) & (frame < first + WIN), wide_mask(a, b), 0.0)
        window = (across[a:b, :] - mean_across[n : n + 1]) * kept * inverse_across[n : n + 1]
        window = window.astype(jnp.bfloat16)
        left = jnp.sum(window.astype(jnp.float32), axis=0, keepdims=True)
        rhs[n, a - k : b - k, :size] = window
        at = n // 16 * 16
        left = jnp.where(iota((16, size), 0) + at == n, -left, 0.0)
        rhs[n, LANES + at : LANES + at + 16, :size] = left.astype(jnp.bfloat16)
    whole = (across[...] - mean_across[SPAN : SPAN + 1]) * wide_mask(0, frames)
    whole = (whole * inverse_across[SPAN : SPAN + 1]).astype(jnp.bfloat16)
    left = jnp.sum(whole.astype(jnp.float32), axis=0, keepdims=True)
    whole_rhs[:frames, :size] = whole
    left = jnp.where((select == SPAN) | (select == 32 + SPAN), -left, 0.0)
    whole_rhs[frames:, :size] = left.astype(jnp.bfloat16)

    scale = jnp.sqrt(total_valid - 3.0) * 0.5

    def compare(slot):
        both = mm(lhs[0], whole_rhs[...])
        out[1, slot] = (scale * log_ratio(both[:, :size] * both[:, size:])).astype(jnp.bfloat16)
        acc1[...] = jnp.zeros_like(acc1)
        acc2[...] = jnp.zeros_like(acc2)
        group = 4

        def step(i, carry):
            first = second = None
            for g in range(group):
                n = i * group + g
                k = n * STRIDE // HALF
                at = pl.ds(pl.multiple_of(k // 2 * LANES, LANES), LANES)
                left = jnp.concatenate([lhs[k % 2, :, at], lhs[0, :, frames:]], axis=1)
                both = mm(left, rhs[n])
                z = log_ratio(both[:, :size] * both[:, size:])
                first = z if g == 0 else first + z
                second = z * z if g == 0 else second + z * z
            acc1[...] += first
            acc2[...] += second
            return carry

        lax.fori_loop(0, NWIN // group, step, 0)
        moment = acc1[...] * (0.5 / NWIN)
        spread = acc2[...] * (0.25 / NWIN) - moment * moment
        out[0, slot] = ((WIN - 3) * spread).astype(jnp.bfloat16)

    compare(me_b)
    for d in range(1, n_blk):
        row_copies[d - 1].wait_recv()
        stat_copies[d - 1].wait_recv()
        load_target(others[d - 1], other_stats[d - 1])
        compare(lax.rem(me_b + n_blk - d, n_blk))

    for copy in seed_copies + row_copies + stat_copies:
        copy.wait_send()


def solution(mesh):
    n_blk, n_wide = mesh.shape["blk"], mesh.shape["wide"]

    def body(series, scrub_mask, seed_index):
        rows, frames = series.shape
        own = seed_index.shape[0]
        size = n_wide * own
        low = (frames // LANES + 1) // 2 * LANES
        hbm = pl.BlockSpec(memory_space=pltpu.HBM)
        out = pl.pallas_call(
            functools.partial(kernel, n_blk, n_wide),
            out_shape=jax.ShapeDtypeStruct((2, n_blk, rows, size), jnp.bfloat16),
            in_specs=[hbm, hbm, hbm],
            out_specs=pl.BlockSpec(memory_space=pltpu.VMEM),
            scratch_shapes=[
                pltpu.VMEM((rows, frames), jnp.bfloat16),
                pltpu.VMEM((frames,), jnp.int32),
                pltpu.SMEM((own,), jnp.int32),
                pltpu.VMEM((2 * own, low), jnp.bfloat16),
                pltpu.VMEM((n_wide - 1, 2 * own, low), jnp.bfloat16),
                pltpu.VMEM((n_blk - 1, rows, frames), jnp.bfloat16),
                pltpu.VMEM((rows, LANES), jnp.bfloat16),
                pltpu.VMEM((n_blk - 1, rows, LANES), jnp.bfloat16),
                pltpu.VMEM((frames, 2 * LANES), jnp.bfloat16),
                pltpu.VMEM((frames, frames), jnp.bfloat16),
                pltpu.VMEM((size, frames), jnp.float32),
                pltpu.VMEM((size, LANES), jnp.float32),
                pltpu.VMEM((frames, size), jnp.float32),
                pltpu.VMEM((frames, LANES), jnp.float32),
                pltpu.VMEM((NWIN, 2 * LANES, 2 * size), jnp.bfloat16),
                pltpu.VMEM((frames + LANES, 2 * size), jnp.bfloat16),
                pltpu.VMEM((2, rows, frames + LANES), jnp.bfloat16),
                pltpu.VMEM((rows, size), jnp.float32),
                pltpu.VMEM((rows, size), jnp.float32),
                pltpu.SemaphoreType.DMA((3,)),
                pltpu.SemaphoreType.DMA((n_wide - 1,)),
                pltpu.SemaphoreType.DMA((n_wide - 1,)),
                pltpu.SemaphoreType.DMA((n_blk - 1,)),
                pltpu.SemaphoreType.DMA((n_blk - 1,)),
                pltpu.SemaphoreType.DMA((n_blk - 1,)),
                pltpu.SemaphoreType.DMA((n_blk - 1,)),
            ],
            compiler_params=pltpu.CompilerParams(
                collective_id=0, has_side_effects=True, vmem_limit_bytes=63 * 2**20
            ),
            cost_estimate=pl.CostEstimate(
                flops=n_blk * rows * size * 2 * 1800, bytes_accessed=2**20, transcendentals=0
            ),
        )(series, scrub_mask, seed_index)
        return out[0], out[1]

    in_specs = (P(("blk", "wide"), None), P(), P(("blk", "wide")))
    out_specs = (P(None, "wide", "blk"), P(None, "wide", "blk"))
    return jax.shard_map(body, mesh=mesh, in_specs=in_specs, out_specs=out_specs, check_vma=False)
```

time: 22.5 us -> 19.8 us (0.88)
  local copies, waits for them, and re-layouts: 3.55 us -> 1.62 us
  Pallas kernels: 17.9 us -> 17.3 us
    unnamed x8 -> x0, local copies, waits for them, and re-layouts: 3.55 us -> none
    squeeze x0 -> x1, local copies, waits for them, and re-layouts: none -> 1.62 us  [body(): return (out[0], out[1])]
    pallas_call x1, Pallas kernels: 17.9 us -> 17.3 us  [body(): pl.pallas_call(functools.partial(kernel, n_blk, n_wide), out_shape=jax.Sh...]
where the time goes in v2:
time: 19.8 us; the launch traced here: 19.6 us
  Pallas kernels  17.3 us (87%)
  local copies, waits for them, and re-layouts  1.62 us (8%)
  between operations  0.64 us (3%)
    pallas_call x1, Pallas kernels, body(): pl.pallas_call(functools.partial(kernel, n_blk, n_wide), out_shape=jax.Sh...  17.3 us
    squeeze x1, local copies, waits for them, and re-layouts, body(): return (out[0], out[1])  1.62 us

profile of v2, /device:TPU:0, one launch (start us, length us, event | category | flops | bytes accessed | tf_op | source)
XLA Modules:
  0.0 19.6 jit_solution(17708079370313079303)
XLA Ops:
  0.6 17.3 %shard_map.50 = bf16[2,2,176,128]{3,2,1,0:T(8,128)(2,1)} custom-call(bf16[176,640]{1,0:T(8,128)(2,1)} %series_hbm.1, s32[640]{0:T(1024)} %mask_hbm.1, s32[8]{0:T(128)} %seed_hbm.1), custom_call_target="tpu_custom_call" | custom-call | flops 162201600 | bytes 1048576 | tf_op jit(solution)/shard_map/pallas_call | solution.py:266
  18.0 1.6 %slice_bitcast_fusion = (bf16[2,176,128]{2,1,0:T(8,128)(2,1)}, bf16[2,176,128]{2,1,0:T(8,128)(2,1)}) fusion(bf16[2,2,176,128]{3,2,1,0:T(8,128)(2,1)} %shard_map.50), kind=kLoop, calls=%fused_computation | loop fusion | bytes 360448 | tf_op jit(solution)/shard_map/squeeze | solution.py:306

commit v3 on v2

--- a/solution.py
+++ b/solution.py
@@ -63,10 +63,11 @@
     for copy in loads:
         copy.start()
     barrier = pltpu.get_barrier_semaphore()
-    for d in range(1, n_wide):
-        pl.semaphore_signal(
-            barrier, inc=1, device_id=(me_b, lax.rem(me_w + d, n_wide)), device_id_type=MESH
-        )
+    half = n_wide // 2
+    sibling = me_w + 1 - 2 * lax.rem(me_w, 2)
+    peers = [lax.rem(me_w + 2 * d, n_wide) for d in range(1, half)]
+    for peer in [sibling] + peers:
+        pl.semaphore_signal(barrier, inc=1, device_id=(me_b, peer), device_id_type=MESH)
     for d in range(1, n_blk):
         pl.semaphore_signal(
             barrier, inc=1, device_id=(lax.rem(me_b + d, n_blk), me_w), device_id_type=MESH
@@ -124,16 +125,19 @@
     block = jnp.where(iota((2 * own, low), 0) < own, picked[:, :low], tail)
     seed_block[...] = block.astype(jnp.bfloat16)
 
-    pl.semaphore_wait(barrier, n_wide + n_blk - 2)
-    seed_copies = []
-    for d in range(1, n_wide):
+    pl.semaphore_wait(barrier, half + n_blk - 1)
+
+    def send_seeds(source, slot, target):
         copy = pltpu.make_async_remote_copy(
-            src_ref=seed_block, dst_ref=panel.at[d - 1],
-            send_sem=seed_send.at[d - 1], recv_sem=seed_recv.at[d - 1],
-            device_id=(me_b, lax.rem(me_w + d, n_wide)), device_id_type=MESH,
+            src_ref=source, dst_ref=panel.at[slot],
+            send_sem=seed_send.at[slot], recv_sem=seed_recv.at[slot],
+            device_id=(me_b, target), device_id_type=MESH,
         )
         copy.start()
-        seed_copies.append(copy)
+        return copy
+
+    direct = [send_seeds(seed_block, d, peers[d]) for d in range(half - 1)]
+    passed = [send_seeds(seed_block, half - 1, sibling)]
 
     def to_group(source, buffer, send, recv):
         copies = []
@@ -181,10 +185,15 @@
         seeds[at, low:] = values[own:, :high]
         seed_stats[at, :] = values[own:, high:]
 
+    for d in range(half - 1):
+        direct[d].wait_recv()
+        passed.append(send_seeds(panel.at[d], half + d, sibling))
     unpack(seed_block[...], me_w)
-    for d in range(1, n_wide):
-        seed_copies[d - 1].wait_recv()
-        unpack(panel[d - 1], lax.rem(me_w + n_wide - d, n_wide))
+    for d in range(half - 1):
+        unpack(panel[d], lax.rem(me_w + n_wide - 2 * (d + 1), n_wide))
+    for d in range(half):
+        passed[d].wait_recv()
+        unpack(panel[half - 1 + d], lax.rem(sibling + n_wide - 2 * d, n_wide))
 
     across[...] = seeds[...].T
     stat_across = seed_stats[...].T
@@ -250,8 +259,19 @@
         load_target(others[d - 1], other_stats[d - 1])
         compare(lax.rem(me_b + n_blk - d, n_blk))
 
-    for copy in seed_copies + row_copies + stat_copies:
+    for copy in direct + passed + row_copies + stat_copies:
         copy.wait_send()
+
+
+def deliver(both, dispersion, statistic, sem):
+    copies = [
+        pltpu.make_async_copy(both.at[0], dispersion, sem.at[0]),
+        pltpu.make_async_copy(both.at[1], statistic, sem.at[1]),
+    ]
+    for copy in copies:
+        copy.start()
+    for copy in copies:
+        copy.wait()
 
 
 def solution(mesh):
@@ -303,7 +323,15 @@
                 flops=n_blk * rows * size * 2 * 1800, bytes_accessed=2**20, transcendentals=0
             ),
         )(series, scrub_mask, seed_index)
-        return out[0], out[1]
+        half = jax.ShapeDtypeStruct((n_blk, rows, size), jnp.bfloat16)
+        return pl.pallas_call(
+            deliver,
+            out_shape=(half, half),
+            in_specs=[hbm],
+            out_specs=(hbm, hbm),
+            scratch_shapes=[pltpu.SemaphoreType.DMA((2,))],
+            compiler_params=pltpu.CompilerParams(vmem_limit_bytes=63 * 2**20),
+        )(out)
 
     in_specs = (P(("blk", "wide"), None), P(), P(("blk", "wide")))
     out_specs = (P(None, "wide", "blk"), P(None, "wide", "blk"))

time: 19.8 us -> 24.1 us (1.22)
  Pallas kernels: 17.3 us -> 23.3 us
  local copies, waits for them, and re-layouts: 1.62 us -> 0 us
    pallas_call x0 -> x1, Pallas kernels: none -> 6.58 us  [body(): pl.pallas_call(deliver, out_shape=(half, half), in_specs=[hbm], out_specs...]
    squeeze x1 -> x0, local copies, waits for them, and re-layouts: 1.62 us -> none  [body(): return (out[0], out[1])]
    pallas_call x1, Pallas kernels: 17.3 us -> 16.7 us  [body(): pl.pallas_call(functools.partial(kernel, n_blk, n_wide), out_shape=jax.Sh...]
where the time goes in v3:
time: 24.1 us; the launch traced here: 23.9 us
  Pallas kernels  23.3 us (97%)
  between operations  0.64 us (3%)
    pallas_call x1, Pallas kernels, body(): pl.pallas_call(functools.partial(kernel, n_blk, n_wide), out_shape=jax.Sh...  16.7 us
    pallas_call x1, Pallas kernels, body(): pl.pallas_call(deliver, out_shape=(half, half), in_specs=[hbm], out_specs...  6.58 us

profile of v3, /device:TPU:0, one launch (start us, length us, event | category | flops | bytes accessed | tf_op | source)
XLA Modules:
  0.0 23.9 jit_solution(16870168667038901569)
XLA Ops:
  0.6 16.7 %shard_map.50.both = bf16[2,2,176,128]{3,2,1,0:T(8,128)(2,1)} custom-call(bf16[176,640]{1,0:T(8,128)(2,1)} %series_hbm.1, s32[640]{0:T(1024)} %mask_hbm.1, s32[8]{0:T(128)} %seed_hbm.1), custom_call_target="tpu_custom_call" | custom-call | flops 162201600 | bytes 1048576 | tf_op jit(solution)/shard_map/pallas_call | solution.py:286
  17.4 6.6 %shard_map.51 = (bf16[2,176,128]{2,1,0:T(8,128)(2,1)}, bf16[2,176,128]{2,1,0:T(8,128)(2,1)}) custom-call(bf16[2,2,176,128]{3,2,1,0:T(8,128)(2,1)} %shard_map.50.both), custom_call_target="tpu_custom_call" | custom-call | tf_op jit(solution)/shard_map/pallas_call | solution.py:327

commit v4 on v3

--- a/solution.py
+++ b/solution.py
@@ -139,19 +139,21 @@
     direct = [send_seeds(seed_block, d, peers[d]) for d in range(half - 1)]
     passed = [send_seeds(seed_block, half - 1, sibling)]
 
-    def to_group(source, buffer, send, recv):
-        copies = []
-        for d in range(1, n_blk):
-            copy = pltpu.make_async_remote_copy(
-                src_ref=source, dst_ref=buffer.at[d - 1],
-                send_sem=send.at[d - 1], recv_sem=recv.at[d - 1],
-                device_id=(lax.rem(me_b + d, n_blk), me_w), device_id_type=MESH,
-            )
-            copy.start()
-            copies.append(copy)
-        return copies
-
-    row_copies = to_group(series, others, row_send, row_recv)
+    def to_group(source, buffer, send, recv, d):
+        return pltpu.make_async_remote_copy(
+            src_ref=source, dst_ref=buffer.at[d - 1],
+            send_sem=send.at[d - 1], recv_sem=recv.at[d - 1],
+            device_id=(lax.rem(me_b + d, n_blk), me_w), device_id_type=MESH,
+        )
+
+    def row_copy(d):
+        return to_group(series, others, row_send, row_recv, d)
+
+    def stat_copy(d):
+        return to_group(own_stat, other_stats, stat_send, stat_recv, d)
+
+    for d in range(1, n_blk):
+        row_copy(d).start()
 
     def load_target(block16, stat):
         lhs[0, :, :frames] = block16
@@ -160,7 +162,8 @@
         lhs[0, :, frames:] = stat
 
     own_stat[...] = stats(series[...].astype(jnp.float32)).astype(jnp.bfloat16)
-    stat_copies = to_group(own_stat, other_stats, stat_send, stat_recv)
+    for d in range(1, n_blk):
+        stat_copy(d).start()
     load_target(series[...], own_stat[...])
 
     select = iota((LANES, size), 0)
@@ -228,50 +231,42 @@
     def compare(slot):
         both = mm(lhs[0], whole_rhs[...])
         out[1, slot] = (scale * log_ratio(both[:, :size] * both[:, size:])).astype(jnp.bfloat16)
-        acc1[...] = jnp.zeros_like(acc1)
-        acc2[...] = jnp.zeros_like(acc2)
         group = 4
-
-        def step(i, carry):
+        for start in range(0, NWIN, group):
             first = second = None
-            for g in range(group):
-                n = i * group + g
+            for n in range(start, start + group):
                 k = n * STRIDE // HALF
-                at = pl.ds(pl.multiple_of(k // 2 * LANES, LANES), LANES)
+                at = slice(k // 2 * LANES, k // 2 * LANES + LANES)
                 left = jnp.concatenate([lhs[k % 2, :, at], lhs[0, :, frames:]], axis=1)
                 both = mm(left, rhs[n])
                 z = log_ratio(both[:, :size] * both[:, size:])
-                first = z if g == 0 else first + z
-                second = z * z if g == 0 else second + z * z
-            acc1[...] += first
-            acc2[...] += second
-            return carry
-
-        lax.fori_loop(0, NWIN // group, step, 0)
+                first = z if n == start else first + z
+                second = z * z if n == start else second + z * z
+            acc1[...] = first if start == 0 else acc1[...] + first
+            acc2[...] = second if start == 0 else acc2[...] + second
         moment = acc1[...] * (0.5 / NWIN)
         spread = acc2[...] * (0.25 / NWIN) - moment * moment
         out[0, slot] = ((WIN - 3) * spread).astype(jnp.bfloat16)
 
     compare(me_b)
-    for d in range(1, n_blk):
-        row_copies[d - 1].wait_recv()
-        stat_copies[d - 1].wait_recv()
+
+    def other(d, carry):
+        row_copy(d).wait_recv()
+        stat_copy(d).wait_recv()
         load_target(others[d - 1], other_stats[d - 1])
         compare(lax.rem(me_b + n_blk - d, n_blk))
-
-    for copy in direct + passed + row_copies + stat_copies:
+        return carry
+
+    if n_blk == 2:
+        other(1, 0)
+    else:
+        lax.fori_loop(1, n_blk, other, 0)
+
+    for copy in direct + passed:
         copy.wait_send()
-
-
-def deliver(both, dispersion, statistic, sem):
-    copies = [
-        pltpu.make_async_copy(both.at[0], dispersion, sem.at[0]),
-        pltpu.make_async_copy(both.at[1], statistic, sem.at[1]),
-    ]
-    for copy in copies:
-        copy.start()
-    for copy in copies:
-        copy.wait()
+    for d in range(1, n_blk):
+        row_copy(d).wait_send()
+        stat_copy(d).wait_send()
 
 
 def solution(mesh):
@@ -323,15 +318,7 @@
                 flops=n_blk * rows * size * 2 * 1800, bytes_accessed=2**20, transcendentals=0
             ),
         )(series, scrub_mask, seed_index)
-        half = jax.ShapeDtypeStruct((n_blk, rows, size), jnp.bfloat16)
-        return pl.pallas_call(
-            deliver,
-            out_shape=(half, half),
-            in_specs=[hbm],
-            out_specs=(hbm, hbm),
-            scratch_shapes=[pltpu.SemaphoreType.DMA((2,))],
-            compiler_params=pltpu.CompilerParams(vmem_limit_bytes=63 * 2**20),
-        )(out)
+        return out[0], out[1]
 
     in_specs = (P(("blk", "wide"), None), P(), P(("blk", "wide")))
     out_specs = (P(None, "wide", "blk"), P(None, "wide", "blk"))

time: 24.1 us -> 18.3 us (0.76)
  Pallas kernels: 23.3 us -> 15.8 us
  local copies, waits for them, and re-layouts: 0 us -> 1.62 us
    pallas_call x1 -> x0, Pallas kernels: 6.58 us -> none  [body(): pl.pallas_call(deliver, out_shape=(half, half), in_specs=[hbm], out_specs...]
    squeeze x0 -> x1, local copies, waits for them, and re-layouts: none -> 1.62 us  [body(): return (out[0], out[1])]
    pallas_call x1, Pallas kernels: 16.7 us -> 15.8 us  [body(): pl.pallas_call(functools.partial(kernel, n_blk, n_wide), out_shape=jax.Sh...]
where the time goes in v4:
time: 18.3 us; the launch traced here: 18.1 us
  Pallas kernels  15.8 us (86%)
  local copies, waits for them, and re-layouts  1.62 us (9%)
  between operations  0.64 us (3%)
    pallas_call x1, Pallas kernels, body(): pl.pallas_call(functools.partial(kernel, n_blk, n_wide), out_shape=jax.Sh...  15.8 us
    squeeze x1, local copies, waits for them, and re-layouts, body(): return (out[0], out[1])  1.62 us

profile of v4, /device:TPU:0, one launch (start us, length us, event | category | flops | bytes accessed | tf_op | source)
XLA Modules:
  0.0 18.1 jit_solution(5570407644286411173)
XLA Ops:
  0.6 15.8 %shard_map.50 = bf16[2,2,176,128]{3,2,1,0:T(8,128)(2,1)} custom-call(bf16[176,640]{1,0:T(8,128)(2,1)} %series_hbm.1, s32[640]{0:T(1024)} %mask_hbm.1, s32[8]{0:T(128)} %seed_hbm.1), custom_call_target="tpu_custom_call" | custom-call | flops 162201600 | bytes 1048576 | tf_op jit(solution)/shard_map/pallas_call | solution.py:281
  16.5 1.6 %slice_bitcast_fusion = (bf16[2,176,128]{2,1,0:T(8,128)(2,1)}, bf16[2,176,128]{2,1,0:T(8,128)(2,1)}) fusion(bf16[2,2,176,128]{3,2,1,0:T(8,128)(2,1)} %shard_map.50), kind=kLoop, calls=%fused_computation | loop fusion | bytes 360448 | tf_op jit(solution)/shard_map/squeeze | solution.py:321
